TPU v7x, 32 devices: a whole 2x2x4 slice. The times are simulated.
32 devices in a mesh: grp: 2 (over x), row: 8 (over z, y), col: 2 (over core).
Axes of the slice: x: 2, y: 2, z: 4, core: 2. Of those that a mesh axis runs over, the one named last changes fastest.
Arguments:
- activations: bfloat16 [128, 8192], P(('grp', 'row', 'col')), parts along dimension 0, may hold values from -2 to 2
- out_grad: bfloat16 [128, 49152], P(('grp', 'row'), 'col'), parts along dimension 0, may hold values from -6 to 6
- weights: bfloat16 [64, 256, 128, 128], P('row', 'col'), may hold values from -0.0390625 to 0.0390625
- counts: int32 [64, 2], P('row', 'col'), may hold values from 64 to 128, as said below
- col_index: int32 [64, 256], P('row', 'col'), may hold values from 0 to 383, as said below
Outputs:
- grad_input: bfloat16 [128, 8192], P(('grp', 'row', 'col')), parts along dimension 0
- grad_weight: bfloat16 [128, 256, 128, 128], P(('grp', 'row'), 'col'), parts along dimension 0
There are 2 independent parts, one for each index of `grp`. A program takes and returns all parts, laid end to end along the dimension named above; an argument that names none is the same for every part. Nothing has to cross between parts.
Inputs may be any that keep to these rules, and one draw needn't show every extreme that they name: `counts`: each entry lies between 64 and 128; in every draw at least one block row has exactly 128 kept blocks in one half. `col_index`: slots h * 128 to (h + 1) * 128 - 1 of a block row hold block columns h * 192 to (h + 1) * 192 - 1; its first counts[i, h] slots hold distinct columns in ascending order, and the remaining slots repeat the first of them.
All inputs are finite; a program needn't handle non-finite values.
Results may differ from a plain program's by a relative error of at most 0.001.
Values may be sent and summed in bfloat16 or wider, within the bound.
A program may use at most 192 MiB of HBM per device.

v0:
```python
import jax
import jax.numpy as jnp
from jax import lax
from jax.sharding import PartitionSpec as P


def local(activations, out_grad, weights, counts, col_index):
    block_size = weights.shape[-1]
    rows_here = weights.shape[0]
    slot_count = weights.shape[1]
    half_blocks = out_grad.shape[1] // block_size
    local_index = col_index - lax.axis_index("col") * half_blocks
    alive_slots = lax.broadcasted_iota(jnp.int32, (rows_here, slot_count), 1) < counts
    masked_w = jnp.where(alive_slots[:, :, None, None], weights, jnp.zeros((), weights.dtype))
    pair_rows = lax.all_gather(activations, "col", axis=0, tiled=True)
    act_panel = lax.all_to_all(pair_rows, "row", split_axis=1, concat_axis=0, tiled=True)
    token_count = act_panel.shape[0]
    x_blocks = act_panel.reshape(token_count, rows_here, block_size)
    flat_index = local_index.reshape(rows_here * slot_count)
    shard_rows = lax.all_gather(out_grad, "row", axis=0, tiled=True)
    width = shard_rows.shape[0]
    columns = jnp.take(shard_rows.reshape(width, half_blocks, block_size), flat_index, axis=1)
    columns = columns.reshape(width, rows_here, slot_count, block_size)
    acc_w = jnp.einsum("tbk,tbsn->bskn", x_blocks, columns, preferred_element_type=jnp.float32)
    partial_value = jnp.einsum(
        "tbsn,bskn->tbk", columns, masked_w, preferred_element_type=jnp.float32
    )
    acc_x = partial_value.reshape(width, rows_here * block_size)
    grad_weight = jnp.where(alive_slots[:, :, None, None], acc_w, jnp.float32(0.0)).astype(
        jnp.bfloat16
    )
    spread = lax.all_to_all(acc_x, "row", split_axis=0, concat_axis=1, tiled=True)
    result = lax.psum_scatter(spread, "col", scatter_dimension=0, tiled=True)
    return (result.astype(jnp.bfloat16), grad_weight)


def solution(mesh):
    return jax.shard_map(
        local,
        mesh=mesh,
        in_specs=(
            P(("grp", "row", "col"), None),
            P(("grp", "row"), "col"),
            P("row", "col", None, None),
            P("row", "col"),
            P("row", "col"),
        ),
        out_specs=(P(("grp", "row", "col"), None), P(("grp", "row"), "col", None, None)),
        check_vma=False,
    )
```

profile of v0, /device:TPU:0, one launch (start us, length us, event | category | flops | bytes accessed | tf_op | source)
XLA Modules:
  0.0 193.5 jit_solution(2939366868606633031)
XLA Ops:
  7.2 0.0 all-gather.3.cloned.1.call-start
  7.2 0.7 all-gather.3.cloned.1.call-update
  7.9 2.2 %all-gather = bf16[2,4,8192]{2,1,0:T(4,128)(2,1)S(1)} all-gather(bf16[1,4,8192]{2,1,0:T(4,128)(2,1)} %bitcast.34), channel_id=1, replica_groups=mesh['grp'=2,'row'=8,'col'=2] {'col'}, dimensions={0}, use_global_device_ids=true | all-gather | bytes 196608 | tf_op jit(solution)/shard_map/all_gather | solution.py:15
  10.1 0.1 all_to_all.30
  10.2 0.7 copy.24
  10.9 7.2 %all-to-all-start.1 = ((bf16[8,8,1024]{2,0,1:T(8,128)(2,1)}), bf16[8,8,1024]{2,0,1:T(8,128)(2,1)S(1)}, u32[]{:S(2)}, u32[]{:S(2)}) async-start(bf16[8,8,1024]{2,0,1:T(8,128)(2,1)} %copy.24), calls=%async_computation.1 | async-start | bytes 262144 | tf_op jit(solution)/shard_map/all_to_all | solution.py:16
  18.1 0.7 compare_and_fusion
  18.8 0.7 iota_compare_fusion
  19.5 1.2 dynamic-slice
  21.4 4.2 %all-to-all-done.1 = bf16[8,8,1024]{2,0,1:T(8,128)(2,1)S(1)} async-done(((bf16[8,8,1024]{2,0,1:T(8,128)(2,1)}), bf16[8,8,1024]{2,0,1:T(8,128)(2,1)S(1)}, u32[]{:S(2)}, u32[]{:S(2)}) %all-to-all-start.1) | async-done | bytes 131104 | tf_op jit(solution)/shard_map/all_to_all | solution.py:16
  25.7 47.5 %all-gather.3.cloned.1.call-done = bf16[64,24576]{1,0:T(8,128)(2,1)} async-done(((bf16[8,24576]{1,0:T(8,128)(2,1)}), bf16[64,24576]{1,0:T(8,128)(2,1)}) %all-gather.3.cloned.1.call-update) | async-done | bytes 3145744 | tf_op jit(solution)/shard_map/all_gather | solution.py:20
  73.2 2.8 %copy_bitcast_fusion = bf16[64,192,128]{2,0,1:T(8,128)(2,1)S(1)} fusion(bf16[64,24576]{1,0:T(8,128)(2,1)} %all-gather.3.cloned.1.call-done), kind=kLoop, calls=%fused_computation.10 | loop fusion | bytes 6291456 | tf_op jit(solution)/shard_map/reshape | solution.py:22
  76.0 13.4 %gather_fusion = bf16[1024,64,128]{2,1,0:T(8,128)(2,1)} fusion(bf16[64,192,128]{2,0,1:T(8,128)(2,1)S(1)} %copy_bitcast_fusion, s32[1024]{0:T(1024)S(1)} %broadcast_clamp_fusion), kind=kCustom, calls=%fused_computation | custom fusion | bytes 33558528 | tf_op jit(solution)/shard_map/jit(_take)/gather | solution.py:22
  89.3 19.2 %fusion.7 = f32[64,8,128]{2,0,1:T(8,128)S(1)} fusion(bf16[64,8,128,128]{3,0,2,1:T(8,128)(2,1)} %bitcast.29, pred[8,128]{1,0:T(8,128)(4,1)S(1)} %get-tuple-element.10, bf16[8,128,128,128]{3,2,1,0:T(8,128)(2,1)} %param.7, pred[8,128]{1,0:T(8,128)(4,1)S(1)} %iota_compare_fusion), kind=kOutput, calls=%fused_computation.11 | convolution fusion | flops 2172649472 | bytes 50595840 | tf_op jit(solution)/shard_map/tbsn,bskn->tbk/dot_general | solution.py:25
  108.5 0.2 copy.23
  108.7 0.7 all_to_all.26
  109.4 3.4 %all-to-all-start = ((f32[8,8,1024]{2,1,0:T(8,128)}), f32[8,8,1024]{2,1,0:T(8,128)S(1)}, u32[]{:S(2)}, u32[]{:S(2)}) async-start(f32[8,8,1024]{2,1,0:T(8,128)} %all_to_all.26), calls=%async_computation | async-start | bytes 524288 | tf_op jit(solution)/shard_map/all_to_all | solution.py:32
  112.8 24.9 %fusion = bf16[8,128,128,128]{2,3,1,0:T(8,128)(2,1)} fusion(pred[8,128]{1,0:T(8,128)(4,1)S(1)} %iota_compare_fusion, bf16[64,8,128,128]{3,0,2,1:T(8,128)(2,1)} %bitcast.30, pred[8,128]{1,0:T(8,128)(4,1)S(1)} %get-tuple-element.10, bf16[64,8,128,1]{2,1,0,3:T(8,128)(2,1)S(1)} %bitcast.33), kind=kOutput, calls=%fused_computation.2 | convolution fusion | flops 2189426688 | bytes 50464768 | tf_op jit(solution)/shard_map/tbk,tbsn->bskn/dot_general | solution.py:24
  137.8 44.0 %copy.26 = bf16[8,128,128,128]{3,2,1,0:T(8,128)(2,1)} copy(bf16[8,128,128,128]{2,3,1,0:T(8,128)(2,1)} %fusion) | data formatting | bytes 67108864
  181.8 0.0 all-to-all-done
  181.8 4.2 %all-reduce.2 = bf16[8,8192]{1,0:T(8,128)(2,1)S(1)} all-reduce(f32[8,8192]{1,0:T(8,128)S(1)} %bitcast.31), channel_id=2, replica_groups=mesh['grp'=2,'row'=8,'col'=2] {'col'}, use_global_device_ids=true, to_apply=%region_0.1.clone | all-reduce | flops 65536 | bytes 393216
  186.0 0.7 dynamic-slice_convert_fusion
  (3 shorter events, 0.0 us)
Async XLA Ops:
  7.2 66.0 %all-gather.3.cloned.1.call-start = ((), (), s32[]{:S(2)}) async-start(), calls=%async_computation.2 | async-start | bytes 3538944 | tf_op jit(solution)/shard_map/all_gather | solution.py:20
  10.9 14.7 %all-to-all-start.1 = ((bf16[8,8,1024]{2,0,1:T(8,128)(2,1)}), bf16[8,8,1024]{2,0,1:T(8,128)(2,1)S(1)}, u32[]{:S(2)}, u32[]{:S(2)}) async-start(bf16[8,8,1024]{2,0,1:T(8,128)(2,1)} %copy.24), calls=%async_computation.1 | async-start | bytes 262144 | tf_op jit(solution)/shard_map/all_to_all | solution.py:16
  109.4 72.4 %all-to-all-start = ((f32[8,8,1024]{2,1,0:T(8,128)}), f32[8,8,1024]{2,1,0:T(8,128)S(1)}, u32[]{:S(2)}, u32[]{:S(2)}) async-start(f32[8,8,1024]{2,1,0:T(8,128)} %all_to_all.26), calls=%async_computation | async-start | bytes 524288 | tf_op jit(solution)/shard_map/all_to_all | solution.py:32
Sparse Core Ops, SparseCore 0:
  10.2 62.9 all-gather.2
where the time goes:
time: 195 us; the launch traced here: 193 us
  local copies, waits for them, and re-layouts  63.8 us (33%)
  waiting for transfers between devices  52.4 us (27%)
  matrix products  44.1 us (23%)
  between operations  14.7 us (8%)
  starting transfers between devices  10.6 us (5%)
  blocking collectives  6.37 us (3%)
    all_gather x1, waiting for transfers between devices, local(): shard_rows = lax.all_gather(out_grad, 'row', axis=0, tiled=True)  47.5 us
    unnamed x3, local copies, waits for them, and re-layouts  45.3 us
    dot_general x1, matrix products, local(): jnp.einsum('tbk,tbsn->bskn', x_blocks, columns, preferred_element_type=jn...  24.9 us
    dot_general x1, matrix products, local(): jnp.einsum('tbsn,bskn->tbk', columns, masked_w, preferred_element_type=jn...  19.2 us
    gather x1, local copies, waits for them, and re-layouts, local(): jnp.take(shard_rows.reshape(width, half_blocks, block_size), flat_index,...  13.4 us
    all_to_all x1, starting transfers between devices, local(): lax.all_to_all(pair_rows, 'row', split_axis=1, concat_axis=0, tiled=True)  7.18 us
    all_to_all x1, waiting for transfers between devices, local(): lax.all_to_all(pair_rows, 'row', split_axis=1, concat_axis=0, tiled=True)  4.19 us
    unnamed x1, blocking collectives  4.16 us
  transfers between devices with their start and end apart: 3, of which 2 were waited for; matrix products, arithmetic and copies ran while one was open for 37% of the time, Pallas kernels for 0%

commit v1 on v0

v1 whole, which is shorter than its diff:
```python
import functools

import jax
import jax.numpy as jnp
from jax import lax
from jax.experimental import pallas as pl
from jax.experimental.pallas import tpu as pltpu
from jax.sharding import PartitionSpec as P

MESH = pl.DeviceIdType.MESH
GROUP = 8
AHEAD = 2


def gather_kernel(
    rows,
    chunks,
    inv_ref,
    og_ref,
    xs_ref,
    w_hbm,
    nat_ref,
    xo_ref,
    go_ref,
    raw,
    wbuf,
    acc,
    xr,
    q_send,
    q_recv,
    q_mine,
    obuf,
    orecv,
    w_sem,
    ring_send,
    ring_recv,
    x_send,
    x_recv,
    q_sems,
    o_send,
    o_recv,
):
    half = rows // 2
    here = acc.shape[0]
    slots = w_hbm.shape[0]
    blk = w_hbm.shape[-1]
    tok = og_ref.shape[0]
    tokens = rows * tok
    pairs = raw.shape[1] // chunks
    cols = pairs * 2
    peers = rows * 2
    row = lax.axis_index("row")
    col = lax.axis_index("col")
    me = row * 2 + col
    odd = row % 2
    pos = (1 - odd) * (row // 2) + odd * (rows - 1 - row // 2)

    def row_at(p):
        p = (p + 2 * rows) % rows
        hi = p // half
        return (1 - hi) * (2 * p) + hi * (2 * (rows - 1 - p) + 1)

    barrier = pltpu.get_barrier_semaphore()

    def greet(d, _):
        peer = (me + d) % peers
        pl.semaphore_signal(
            barrier, inc=1, device_id={"row": peer // 2, "col": peer % 2}, device_id_type=MESH
        )
        return 0

    lax.fori_loop(1, peers, greet, 0)
    w_copy = pltpu.make_async_copy(w_hbm, wbuf.at[pl.ds(0, slots)], w_sem)
    w_copy.start()

    def lay_out(q, _):
        both = og_ref[:, pl.ds(pl.multiple_of(q * 2 * blk, 2 * blk), 2 * blk)].astype(jnp.float32)
        raw[row, q] = jnp.concatenate([both[:, :blk], both[:, blk:]], axis=0).astype(raw.dtype)
        return 0

    lax.fori_loop(0, raw.shape[1], lay_out, 0, unroll=4)
    pl.semaphore_wait(barrier, peers - 1)

    def ring_copy(d, k, c):
        origin = row_at(pos - k) if d == 0 else row_at(pos + k)
        target = row_at(pos + 1) if d == 0 else row_at(pos - 1)
        part = raw.at[origin, pl.ds(c * pairs, pairs)]
        return pltpu.make_async_remote_copy(
            src_ref=part,
            dst_ref=part,
            send_sem=ring_send.at[d, k, c],
            recv_sem=ring_recv.at[d, k, c],
            device_id={"row": target},
            device_id_type=MESH,
        )

    def ring_arrival(d, k, c):
        origin = row_at(pos - 1 - k) if d == 0 else row_at(pos + 1 + k)
        target = row_at(pos + 1) if d == 0 else row_at(pos - 1)
        part = raw.at[origin, pl.ds(c * pairs, pairs)]
        return pltpu.make_async_remote_copy(
            src_ref=part,
            dst_ref=part,
            send_sem=ring_send.at[d, k, c],
            recv_sem=ring_recv.at[d, k, c],
            device_id={"row": target},
            device_id_type=MESH,
        )

    def x_copy(d):
        peer = (me + d) % peers
        return pltpu.make_async_remote_copy(
            src_ref=xs_ref.at[peer // 2],
            dst_ref=xr.at[me],
            send_sem=x_send.at[d],
            recv_sem=x_recv.at[d],
            device_id={"row": peer // 2, "col": peer % 2},
            device_id_type=MESH,
        )

    def x_arrival(d):
        peer = (me + peers - d) % peers
        return pltpu.make_async_remote_copy(
            src_ref=xs_ref.at[peer // 2],
            dst_ref=xr.at[peer],
            send_sem=x_send.at[d],
            recv_sem=x_recv.at[d],
            device_id={"row": peer // 2, "col": peer % 2},
            device_id_type=MESH,
        )

    for c in range(min(AHEAD, chunks)):
        for d in (0, 1):
            ring_copy(d, 0, c).start()

    def send_x(d, _):
        x_copy(d).start()
        return 0

    lax.fori_loop(1, peers, send_x, 0)
    xr[me] = xs_ref[row]
    wbuf[slots] = jnp.zeros((blk, blk), wbuf.dtype)
    acc[...] = jnp.zeros_like(acc)

    def hop(t, k):
        c = t - k
        for d in (0, 1):
            ok = (c >= 0) & (c < chunks)
            if k == half - 1:
                ok = ok & (c % 2 == d)

            @pl.when(ok)
            def _():
                ring_arrival(d, k - 1, c).wait_recv()
                ring_copy(d, k, c).start()

    def compute(c):
        def natural(j, _):
            q = c * pairs + j
            both = raw[:, q].astype(jnp.float32).reshape(rows, 2, tok, blk)
            nat_ref[2 * q] = both[:, 0].reshape(tokens, blk).astype(nat_ref.dtype)
            nat_ref[2 * q + 1] = both[:, 1].reshape(tokens, blk).astype(nat_ref.dtype)
            return 0

        lax.fori_loop(0, pairs, natural, 0, unroll=2)

        def group(g, _):
            first = c * cols + g * GROUP
            panel = jnp.concatenate([nat_ref[first + m] for m in range(GROUP)], axis=1)
            for i in range(here):
                blocks = jnp.concatenate(
                    [wbuf[inv_ref[i, first + m]] for m in range(GROUP)], axis=1
                )
                acc[i] += lax.dot_general(
                    blocks, panel, (((1,), (1,)), ((), ())), preferred_element_type=jnp.float32
                )
            return 0

        lax.fori_loop(0, cols // GROUP, group, 0)

    def tick(t, _):
        @pl.when(t + AHEAD < chunks)
        def _():
            for d in (0, 1):
                ring_copy(d, 0, t + AHEAD).start()

        if half > 1:
            hop(t, 1)
        for k in range(half - 1, 1, -1):
            hop(t, k)

        @pl.when(t >= half)
        def _():
            c = t - half

            @pl.when(c == 0)
            def _():
                w_copy.wait()

            for d in (0, 1):
                @pl.when(c % 2 == d)
                def _():
                    ring_arrival(d, half - 1, c).wait_recv()
                    ring_arrival(1 - d, half - 2, c).wait_recv()

            compute(c)

        return 0

    lax.fori_loop(0, chunks + half, tick, 0)

    below = lax.broadcasted_iota(jnp.int32, (rows, 8, blk), 1) < 4
    first_core = (lax.broadcasted_iota(jnp.int32, (rows, 8, blk), 1) * 0 + col) == 0
    zero = jnp.zeros((rows, 8, blk), jnp.float32)

    def tile(i):
        if i >= here:
            return zero
        return jnp.transpose(acc[i], (1, 0)).reshape(rows, tok, blk)

    for i2 in range(q_send.shape[1]):
        a, b = tile(2 * i2), tile(2 * i2 + 1)
        for_first = jnp.where(below, a, pltpu.roll(b, 4, 1))
        for_second = jnp.where(below, pltpu.roll(a, 4, 1), b)
        q_mine[:, i2] = jnp.where(first_core, for_first, for_second)
        q_send[:, i2] = jnp.where(first_core, for_second, for_first)

    swap = pltpu.make_async_remote_copy(
        src_ref=q_send,
        dst_ref=q_recv,
        send_sem=q_sems.at[0],
        recv_sem=q_sems.at[1],
        device_id={"col": 1 - col},
        device_id_type=MESH,
    )
    swap.start()

    def wait_x(d, _):
        x_arrival(d).wait_recv()
        x_copy(d).wait_send()
        return 0

    lax.fori_loop(1, peers, wait_x, 0)
    xo_ref[...] = xr[...]

    def wait_ring(c, _):
        for k in range(half):
            for d in (0, 1):
                if k == half - 1:

                    @pl.when(c % 2 == d)
                    def _():
                        ring_copy(d, k, c).wait_send()

                else:
                    ring_copy(d, k, c).wait_send()
        return 0

    lax.fori_loop(0, chunks, wait_ring, 0)
    swap.wait()
    total = q_mine[...] + q_recv[...]
    obuf[...] = total.reshape(obuf.shape).astype(obuf.dtype)

    def o_copy(d):
        peer = (row + d) % rows
        return pltpu.make_async_remote_copy(
            src_ref=obuf.at[peer],
            dst_ref=orecv.at[row],
            send_sem=o_send.at[d],
            recv_sem=o_recv.at[d],
            device_id={"row": peer},
            device_id_type=MESH,
        )

    def o_arrival(d):
        peer = (row + rows - d) % rows
        return pltpu.make_async_remote_copy(
            src_ref=obuf.at[peer],
            dst_ref=orecv.at[peer],
            send_sem=o_send.at[d],
            recv_sem=o_recv.at[d],
            device_id={"row": peer},
            device_id_type=MESH,
        )

    def send_o(d, _):
        o_copy(d).start()
        return 0

    def wait_o(d, _):
        o_arrival(d).wait_recv()
        o_copy(d).wait_send()
        return 0

    lax.fori_loop(1, rows, send_o, 0)
    orecv[row] = obuf[row]
    lax.fori_loop(1, rows, wait_o, 0)
    go_ref[...] = orecv[...]


def weight_kernel(per_step, wide, idx_ref, cnt_ref, og_ref, x_ref, out_ref):
    i = pl.program_id(0)
    base = pl.program_id(1) * per_step
    count = cnt_ref[i]
    blk = out_ref.shape[-1]
    x = x_ref[0]
    for s in range(0, per_step, wide):
        parts = []
        for m in range(wide):
            slot = base + s + m
            part = og_ref[idx_ref[i, slot]]
            parts.append(jnp.where(slot < count, part, jnp.zeros_like(part)))
        panel = jnp.concatenate(parts, axis=1)
        out = jnp.dot(x, panel, preferred_element_type=jnp.float32).astype(out_ref.dtype)
        for m in range(wide):
            out_ref[0, s + m] = out[:, m * blk : (m + 1) * blk]


def local(rows, activations, out_grad, weights, counts, col_index):
    blk = weights.shape[-1]
    here, slots = weights.shape[:2]
    tok, width = out_grad.shape
    act_tok = activations.shape[0]
    n_cols = width // blk
    tokens = rows * tok
    half = rows // 2
    chunks = n_cols // (2 * GROUP)
    bf16, f32 = jnp.bfloat16, jnp.float32

    index = col_index - lax.axis_index("col") * n_cols
    flat_slot = lax.broadcasted_iota(jnp.int32, (here, slots), 0) * slots
    slot_id = lax.broadcasted_iota(jnp.int32, (here, slots), 1)
    alive = slot_id < counts
    named = jnp.where(alive, index, -1)
    match = named[:, :, None] == lax.broadcasted_iota(jnp.int32, (1, 1, n_cols), 2)
    inverse = jnp.min(
        jnp.where(match, (flat_slot + slot_id)[:, :, None], here * slots), axis=1
    ).astype(jnp.int32)

    x_rows = -(-here * act_tok // 16) * 16
    xs = activations.reshape(act_tok, rows, here, blk).transpose(1, 2, 0, 3)
    xs = xs.reshape(rows, here * act_tok, blk)
    if x_rows != here * act_tok:
        xs = jnp.pad(xs, ((0, 0), (0, x_rows - here * act_tok), (0, 0)))

    here4 = -(-here // 4) * 4
    o_rows = here4 * 4
    q_shape = (rows, here4 // 2, 8, blk)
    vmem = pl.BlockSpec(memory_space=pltpu.VMEM)
    planned = (
        2 * (width * tokens * 2)
        + (here * slots + 1) * blk * blk * 2
        + tok * width * 4
        + 3 * 4 * rows * here4 * 4 * blk
        + 6 * 2 * rows * (2 * x_rows + o_rows) * blk
        + here * blk * max(tokens, 128) * 4
    )
    nat, x_all, g_all = pl.pallas_call(
        functools.partial(gather_kernel, rows, chunks),
        out_shape=(
            jax.ShapeDtypeStruct((n_cols, tokens, blk), bf16),
            jax.ShapeDtypeStruct((rows * 2, x_rows, blk), bf16),
            jax.ShapeDtypeStruct((rows, o_rows, blk), bf16),
        ),
        in_specs=[
            pl.BlockSpec(memory_space=pltpu.SMEM),
            vmem,
            vmem,
            pl.BlockSpec(memory_space=pl.ANY),
        ],
        out_specs=(vmem, vmem, vmem),
        scratch_shapes=[
            pltpu.VMEM((rows, n_cols // 2, 2 * tok, blk), bf16),
            pltpu.VMEM((here * slots + 1, blk, blk), bf16),
            pltpu.VMEM((here, blk, tokens), f32),
            pltpu.VMEM((rows * 2, x_rows, blk), bf16),
            pltpu.VMEM(q_shape, f32),
            pltpu.VMEM(q_shape, f32),
            pltpu.VMEM(q_shape, f32),
            pltpu.VMEM((rows, o_rows, blk), bf16),
            pltpu.VMEM((rows, o_rows, blk), bf16),
            pltpu.SemaphoreType.DMA,
            pltpu.SemaphoreType.DMA((2, half, chunks)),
            pltpu.SemaphoreType.DMA((2, half, chunks)),
            pltpu.SemaphoreType.DMA((rows * 2,)),
            pltpu.SemaphoreType.DMA((rows * 2,)),
            pltpu.SemaphoreType.DMA((2,)),
            pltpu.SemaphoreType.DMA((rows,)),
            pltpu.SemaphoreType.DMA((rows,)),
        ],
        compiler_params=pltpu.CompilerParams(
            collective_id=0,
            has_side_effects=True,
            vmem_limit_bytes=min(planned + (6 << 20), 60 << 20),
        ),
        cost_estimate=pl.CostEstimate(
            flops=2 * here * n_cols * blk * blk * tokens,
            bytes_accessed=weights.size * 2 + 2 * width * tokens * 2,
            transcendentals=0,
        ),
    )(inverse, out_grad, xs, weights.reshape(here * slots, blk, blk))

    x_t = x_all[:, : here * act_tok].reshape(rows * 2, here, act_tok, blk)
    x_t = x_t.transpose(1, 3, 0, 2).reshape(here, blk, tokens)

    per_step, wide = min(32, slots), 4
    grad_weight = pl.pallas_call(
        functools.partial(weight_kernel, per_step, wide),
        out_shape=jax.ShapeDtypeStruct(weights.shape, bf16),
        grid_spec=pltpu.PrefetchScalarGridSpec(
            num_scalar_prefetch=2,
            grid=(here, slots // per_step),
            in_specs=[
                pl.BlockSpec(
                    (n_cols, tokens, blk),
                    lambda i, j, *_: (0, 0, 0),
                    pipeline_mode=pl.Buffered(1),
                ),
                pl.BlockSpec((1, blk, tokens), lambda i, j, *_: (i, 0, 0)),
            ],
            out_specs=pl.BlockSpec((1, per_step, blk, blk), lambda i, j, *_: (i, j, 0, 0)),
        ),
        compiler_params=pltpu.CompilerParams(
            vmem_limit_bytes=n_cols * tokens * blk * 2 + (16 << 20),
        ),
    )(index, counts.reshape(here), nat, x_t)

    g = g_all[:, : here * act_tok].reshape(rows, here, act_tok, blk)
    grad_input = g.transpose(2, 0, 1, 3).reshape(act_tok, rows * here * blk)
    return grad_input, grad_weight


def solution(mesh):
    return jax.shard_map(
        functools.partial(local, mesh.shape["row"]),
        mesh=mesh,
        in_specs=(
            P(("grp", "row", "col"), None),
            P(("grp", "row"), "col"),
            P("row", "col", None, None),
            P("row", "col"),
            P("row", "col"),
        ),
        out_specs=(P(("grp", "row", "col"), None), P(("grp", "row"), "col", None, None)),
        check_vma=False,
    )
```

time: 195 us -> 92.7 us (0.48)
  Pallas kernels: 0 us -> 86.3 us
  local copies, waits for them, and re-layouts: 63.8 us -> 4.24 us
  waiting for transfers between devices: 52.4 us -> 0 us
  matrix products: 44.1 us -> 0 us
  between operations: 14.7 us -> 0.69 us
  starting transfers between devices: 10.6 us -> 0 us
  blocking collectives: 6.37 us -> 0 us
    pallas_call x0 -> x2, Pallas kernels: none -> 86.3 us  [the longest x1 62.9 us: local(): pl.pallas_call(functools.partial(gather_kernel, rows, chunks), out_shape=...]
    all_gather x1 -> x0, waiting for transfers between devices: 47.5 us -> none  [local(): shard_rows = lax.all_gather(out_grad, 'row', axis=0, tiled=True)]
    dot_general x2 -> x0, matrix products: 44.1 us -> none  [the longest x1 24.9 us: local(): jnp.einsum('tbk,tbsn->bskn', x_blocks, columns, preferred_element_type=jn...]
    unnamed x3 -> x7, local copies, waits for them, and re-layouts: 45.3 us -> 2.47 us
    gather x1 -> x0, local copies, waits for them, and re-layouts: 13.4 us -> none  [local(): jnp.take(shard_rows.reshape(width, half_blocks, block_size), flat_index,...]
    all_to_all x2 -> x0, starting transfers between devices: 10.6 us -> none  [the longest x1 7.18 us: local(): lax.all_to_all(pair_rows, 'row', split_axis=1, concat_axis=0, tiled=True)]
    all_to_all x2 -> x0, waiting for transfers between devices: 4.2 us -> none  [the longest x1 4.19 us: local(): lax.all_to_all(pair_rows, 'row', split_axis=1, concat_axis=0, tiled=True)]
    unnamed x1 -> x0, blocking collectives: 4.16 us -> none
  transfers between devices with their start and end apart: 3 -> 0, of which waited for: 2 -> 0; matrix products, arithmetic and copies ran while one was open for 37% -> 0% of each run, Pallas kernels for 0% -> 0%
where the time goes in v1:
time: 92.7 us; the launch traced here: 92.4 us
  Pallas kernels  86.3 us (93%)
  local copies, waits for them, and re-layouts  4.24 us (5%)
  other arithmetic  1.17 us (1%)
    pallas_call x1, Pallas kernels, local(): pl.pallas_call(functools.partial(gather_kernel, rows, chunks), out_shape=...  62.9 us
    pallas_call x1, Pallas kernels, local(): pl.pallas_call(functools.partial(weight_kernel, per_step, wide), out_shap...  23.4 us
    unnamed x7, local copies, waits for them, and re-layouts  2.47 us

profile of v1, /device:TPU:0, one launch (start us, length us, event | category | flops | bytes accessed | tf_op | source)
XLA Modules:
  0.0 92.4 jit_solution(13730802374790435037)
XLA Ops:
  0.6 0.0 copy-start.2
  0.7 0.8 fusion
  1.4 0.4 select_reduce_fusion.inv_ref
  1.8 0.0 copy-start
  1.8 1.0 %copy-done = bf16[8,24576]{1,0:T(8,128)(2,1)S(1)} copy-done((bf16[8,24576]{1,0:T(8,128)(2,1)S(1)}, bf16[8,24576]{1,0:T(8,128)(2,1)}, u32[]{:S(2)}) %copy-start) | copy-done | bytes 393240
  2.8 0.0 copy-start.1
  2.8 0.8 copy-done.1
  3.7 62.9 %shard_map.68 = (bf16[192,64,128]{2,1,0:T(8,128)(2,1)S(1)}, bf16[16,32,128]{2,1,0:T(8,128)(2,1)S(1)}, bf16[8,32,128]{2,1,0:T(8,128)(2,1)S(1)}) custom-call(s32[8,192]{1,0:T(8,128)S(1)} %select_reduce_fusion.inv_ref, bf16[8,24576]{1,0:T(8,128)(2,1)S(1)} %copy-done, bf16[8,32,128]{2,1,0:T(8,128)(2,1)S(1)} %bitcast.17, bf16[1024,128,128]{2,1,0:T(8,128)(2,1)} %bitcast.21), custom_call_target="tpu_custom_call" | custom-call | flops 3221225472 | bytes 39845888 | tf_op jit(solution)/shard_map/pallas_call | solution.py:358
  66.6 0.7 copy.16
  67.3 1.1 %copy.17.x_ref = bf16[8,128,64]{2,1,0:T(8,128)(2,1)S(1)} copy(bf16[8,128,64]{1,0,2:T(8,128)(2,1)} %bitcast.22) | data formatting | bytes 262144 | tf_op jit(solution)/shard_map/reshape | solution.py:404
  68.4 0.0 copy-done.2
  68.4 23.4 %shard_map.69 = bf16[8,128,128,128]{3,2,1,0:T(8,128)(2,1)} custom-call(s32[8,128]{1,0:T(8,128)S(1)} %get-tuple-element.9.idx_ref, s32[8]{0:T(128)S(1)} %bitcast.20, bf16[192,64,128]{2,1,0:T(8,128)(2,1)S(1)} %get-tuple-element.6.og_ref, bf16[8,128,64]{2,1,0:T(8,128)(2,1)S(1)} %copy.17.x_ref), custom_call_target="tpu_custom_call" | custom-call | tf_op jit(solution)/shard_map/pallas_call | solution.py:407
  91.8 0.6 copy.19
  (1 shorter events, 0.0 us)
Async XLA Ops:
  0.6 67.7 %copy-start.2 = (s32[8,1]{0,1:T(1,128)S(1)}, s32[8,1]{0,1:T(1,128)}, u32[]{:S(2)}) copy-start(s32[8,1]{0,1:T(1,128)} %param.8) | copy-start | bytes 100
  1.8 1.0 %copy-start = (bf16[8,24576]{1,0:T(8,128)(2,1)S(1)}, bf16[8,24576]{1,0:T(8,128)(2,1)}, u32[]{:S(2)}) copy-start(bf16[8,24576]{1,0:T(8,128)(2,1)} %og_ref.1) | copy-start | bytes 1179652
  2.8 0.8 copy-start.1

commit v2 on v1

--- a/solution.py
+++ b/solution.py
@@ -298,22 +298,47 @@
     go_ref[...] = orecv[...]
 
 
-def weight_kernel(per_step, wide, idx_ref, cnt_ref, og_ref, x_ref, out_ref):
-    i = pl.program_id(0)
-    base = pl.program_id(1) * per_step
-    count = cnt_ref[i]
-    blk = out_ref.shape[-1]
-    x = x_ref[0]
-    for s in range(0, per_step, wide):
-        parts = []
-        for m in range(wide):
-            slot = base + s + m
-            part = og_ref[idx_ref[i, slot]]
-            parts.append(jnp.where(slot < count, part, jnp.zeros_like(part)))
-        panel = jnp.concatenate(parts, axis=1)
-        out = jnp.dot(x, panel, preferred_element_type=jnp.float32).astype(out_ref.dtype)
-        for m in range(wide):
-            out_ref[0, s + m] = out[:, m * blk : (m + 1) * blk]
+def weight_kernel(per_step, wide, depth, idx_ref, cnt_ref, og_ref, x_ref, out_hbm, buf, sems):
+    here, slots = out_hbm.shape[:2]
+    blk = out_hbm.shape[-1]
+    per_row = slots // per_step
+    steps = here * per_row
+
+    def out_copy(t):
+        lane = t % depth
+        return pltpu.make_async_copy(
+            buf.at[lane],
+            out_hbm.at[t // per_row, pl.ds((t % per_row) * per_step, per_step)],
+            sems.at[lane],
+        )
+
+    def step(t, _):
+        i = t // per_row
+        base = (t % per_row) * per_step
+        lane = t % depth
+        count = cnt_ref[i]
+        x = x_ref[i]
+
+        @pl.when(t >= depth)
+        def _():
+            out_copy(t - depth).wait()
+
+        for s in range(0, per_step, wide):
+            parts = []
+            for m in range(wide):
+                slot = base + s + m
+                part = og_ref[idx_ref[i, slot]]
+                parts.append(jnp.where(slot < count, part, jnp.zeros_like(part)))
+            panel = jnp.concatenate(parts, axis=1)
+            out = jnp.dot(x, panel, preferred_element_type=jnp.float32).astype(buf.dtype)
+            for m in range(wide):
+                buf[lane, s + m] = out[:, m * blk : (m + 1) * blk]
+        out_copy(t).start()
+        return 0
+
+    lax.fori_loop(0, steps, step, 0)
+    for t in range(max(0, steps - depth), steps):
+        out_copy(t).wait()
 
 
 def local(rows, activations, out_grad, weights, counts, col_index):
@@ -324,7 +349,7 @@
     n_cols = width // blk
     tokens = rows * tok
     half = rows // 2
-    chunks = n_cols // (2 * GROUP)
+    chunks = n_cols // (4 * GROUP)
     bf16, f32 = jnp.bfloat16, jnp.float32
 
     index = col_index - lax.axis_index("col") * n_cols
@@ -403,23 +428,21 @@
     x_t = x_all[:, : here * act_tok].reshape(rows * 2, here, act_tok, blk)
     x_t = x_t.transpose(1, 3, 0, 2).reshape(here, blk, tokens)
 
-    per_step, wide = min(32, slots), 4
+    per_step, wide, depth = min(128, slots), 8, 2
     grad_weight = pl.pallas_call(
-        functools.partial(weight_kernel, per_step, wide),
+        functools.partial(weight_kernel, per_step, wide, depth),
         out_shape=jax.ShapeDtypeStruct(weights.shape, bf16),
-        grid_spec=pltpu.PrefetchScalarGridSpec(
-            num_scalar_prefetch=2,
-            grid=(here, slots // per_step),
-            in_specs=[
-                pl.BlockSpec(
-                    (n_cols, tokens, blk),
-                    lambda i, j, *_: (0, 0, 0),
-                    pipeline_mode=pl.Buffered(1),
-                ),
-                pl.BlockSpec((1, blk, tokens), lambda i, j, *_: (i, 0, 0)),
-            ],
-            out_specs=pl.BlockSpec((1, per_step, blk, blk), lambda i, j, *_: (i, j, 0, 0)),
-        ),
+        in_specs=[
+            pl.BlockSpec(memory_space=pltpu.SMEM),
+            pl.BlockSpec(memory_space=pltpu.SMEM),
+            vmem,
+            vmem,
+        ],
+        out_specs=pl.BlockSpec(memory_space=pl.ANY),
+        scratch_shapes=[
+            pltpu.VMEM((depth, per_step, blk, blk), bf16),
+            pltpu.SemaphoreType.DMA((depth,)),
+        ],
         compiler_params=pltpu.CompilerParams(
             vmem_limit_bytes=n_cols * tokens * blk * 2 + (16 << 20),
         ),

time: 92.7 us -> 76.3 us (0.82)
  Pallas kernels: 86.3 us -> 70 us
    pallas_call x1, Pallas kernels: 23.4 us -> 15 us  [local(): pl.pallas_call(functools.partial(weight_kernel, per_step, wide, depth), o...]
    pallas_call x1, Pallas kernels: 62.9 us -> 54.9 us  [local(): pl.pallas_call(functools.partial(gather_kernel, rows, chunks), out_shape=...]
where the time goes in v2:
time: 76.3 us; the launch traced here: 76.1 us
  Pallas kernels  70 us (92%)
  local copies, waits for them, and re-layouts  4.24 us (6%)
  other arithmetic  1.17 us (2%)
    pallas_call x1, Pallas kernels, local(): pl.pallas_call(functools.partial(gather_kernel, rows, chunks), out_shape=...  54.9 us
    pallas_call x1, Pallas kernels, local(): pl.pallas_call(functools.partial(weight_kernel, per_step, wide, depth), o...  15 us
    unnamed x7, local copies, waits for them, and re-layouts  2.47 us

profile of v2, /device:TPU:0, one launch (start us, length us, event | category | flops | bytes accessed | tf_op | source)
XLA Modules:
  0.0 76.1 jit_solution(5769711097736153958)
XLA Ops:
  0.6 0.0 copy-start.2
  0.7 0.8 %fusion = (s32[8,128]{1,0:T(8,128)S(1)}, s32[8,128]{1,0:T(8,128)S(1)}, s32[8,128]{1,0:T(8,128)S(1)}) fusion(s32[8]{0:T(128)} %bitcast.19, s32[8,128]{1,0:T(8,128)} %param.9, s32[]{:T(128)S(6)} %mul.10, s32[8]{0:T(128)S(1)} %iota_multiply_fusion), kind=kLoop, calls=%fused_computation.4 | loop fusion | flops 4096 | bytes 16452 | tf_op jit(solution)/shard_map/jit(_where)/select_n | solution.py:359
  1.4 0.4 select_reduce_fusion.inv_ref
  1.8 0.0 copy-start
  1.8 1.0 %copy-done = bf16[8,24576]{1,0:T(8,128)(2,1)S(1)} copy-done((bf16[8,24576]{1,0:T(8,128)(2,1)S(1)}, bf16[8,24576]{1,0:T(8,128)(2,1)}, u32[]{:S(2)}) %copy-start) | copy-done | bytes 393240
  2.8 0.0 copy-start.1
  2.8 0.8 %copy-done.1 = bf16[4,8192]{1,0:T(4,128)(2,1)S(1)} copy-done((bf16[4,8192]{1,0:T(4,128)(2,1)S(1)}, bf16[4,8192]{1,0:T(4,128)(2,1)}, u32[]{:S(2)}) %copy-start.1) | copy-done | bytes 65560
  3.7 54.9 %shard_map.68 = (bf16[192,64,128]{2,1,0:T(8,128)(2,1)S(1)}, bf16[16,32,128]{2,1,0:T(8,128)(2,1)S(1)}, bf16[8,32,128]{2,1,0:T(8,128)(2,1)S(1)}) custom-call(s32[8,192]{1,0:T(8,128)S(1)} %select_reduce_fusion.inv_ref, bf16[8,24576]{1,0:T(8,128)(2,1)S(1)} %copy-done, bf16[8,32,128]{2,1,0:T(8,128)(2,1)S(1)} %bitcast.17, bf16[1024,128,128]{2,1,0:T(8,128)(2,1)} %bitcast.21), custom_call_target="tpu_custom_call" | custom-call | flops 3221225472 | bytes 39845888 | tf_op jit(solution)/shard_map/pallas_call | solution.py:383
  58.6 0.7 copy.16
  59.3 1.1 %copy.17.x_ref = bf16[8,128,64]{2,1,0:T(8,128)(2,1)S(1)} copy(bf16[8,128,64]{1,0,2:T(8,128)(2,1)} %bitcast.22) | data formatting | bytes 262144 | tf_op jit(solution)/shard_map/reshape | solution.py:429
  60.4 0.0 copy-done.2
  60.4 15.0 %shard_map.69 = bf16[8,128,128,128]{3,2,1,0:T(8,128)(2,1)} custom-call(s32[8,128]{1,0:T(8,128)S(1)} %get-tuple-element.9.idx_ref, s32[8]{0:T(128)S(1)} %bitcast.20, bf16[192,64,128]{2,1,0:T(8,128)(2,1)S(1)} %get-tuple-element.6.og_ref, bf16[8,128,64]{2,1,0:T(8,128)(2,1)S(1)} %copy.17.x_ref), custom_call_target="tpu_custom_call" | custom-call | tf_op jit(solution)/shard_map/pallas_call | solution.py:432
  75.5 0.6 copy.19
  (1 shorter events, 0.0 us)
Async XLA Ops:
  0.6 59.8 %copy-start.2 = (s32[8,1]{0,1:T(1,128)S(1)}, s32[8,1]{0,1:T(1,128)}, u32[]{:S(2)}) copy-start(s32[8,1]{0,1:T(1,128)} %param.8) | copy-start | bytes 100
  1.8 1.0 %copy-start = (bf16[8,24576]{1,0:T(8,128)(2,1)S(1)}, bf16[8,24576]{1,0:T(8,128)(2,1)}, u32[]{:S(2)}) copy-start(bf16[8,24576]{1,0:T(8,128)(2,1)} %og_ref.1) | copy-start | bytes 1179652
  2.8 0.8 %copy-start.1 = (bf16[4,8192]{1,0:T(4,128)(2,1)S(1)}, bf16[4,8192]{1,0:T(4,128)(2,1)}, u32[]{:S(2)}) copy-start(bf16[4,8192]{1,0:T(4,128)(2,1)} %param.5) | copy-start | bytes 196612

commit v3 on v2

--- a/solution.py
+++ b/solution.py
@@ -9,7 +9,7 @@
 
 MESH = pl.DeviceIdType.MESH
 GROUP = 8
-AHEAD = 2
+AHEAD = 1
 
 
 def gather_kernel(

time: 76.3 us -> 75.7 us (level)
  no operation moved by 1% of the time
where the time goes in v3:
time: 75.7 us; the launch traced here: 75.4 us
  Pallas kernels  69.3 us (92%)
  local copies, waits for them, and re-layouts  4.24 us (6%)
  other arithmetic  1.17 us (2%)
    pallas_call x1, Pallas kernels, local(): pl.pallas_call(functools.partial(gather_kernel, rows, chunks), out_shape=...  54.3 us
    pallas_call x1, Pallas kernels, local(): pl.pallas_call(functools.partial(weight_kernel, per_step, wide, depth), o...  15 us
    unnamed x7, local copies, waits for them, and re-layouts  2.47 us

profile of v3, /device:TPU:0, one launch (start us, length us, event | category | flops | bytes accessed | tf_op | source)
XLA Modules:
  0.0 75.4 jit_solution(5811967833609433627)
XLA Ops:
  0.6 0.0 copy-start.2
  0.7 0.8 %fusion = (s32[8,128]{1,0:T(8,128)S(1)}, s32[8,128]{1,0:T(8,128)S(1)}, s32[8,128]{1,0:T(8,128)S(1)}) fusion(s32[8]{0:T(128)} %bitcast.19, s32[8,128]{1,0:T(8,128)} %param.9, s32[]{:T(128)S(6)} %mul.10, s32[8]{0:T(128)S(1)} %iota_multiply_fusion), kind=kLoop, calls=%fused_computation.4 | loop fusion | flops 4096 | bytes 16452 | tf_op jit(solution)/shard_map/jit(_where)/select_n | solution.py:359
  1.4 0.4 select_reduce_fusion.inv_ref
  1.8 0.0 copy-start
  1.8 1.0 %copy-done = bf16[8,24576]{1,0:T(8,128)(2,1)S(1)} copy-done((bf16[8,24576]{1,0:T(8,128)(2,1)S(1)}, bf16[8,24576]{1,0:T(8,128)(2,1)}, u32[]{:S(2)}) %copy-start) | copy-done | bytes 393240
  2.8 0.0 copy-start.1
  2.8 0.8 %copy-done.1 = bf16[4,8192]{1,0:T(4,128)(2,1)S(1)} copy-done((bf16[4,8192]{1,0:T(4,128)(2,1)S(1)}, bf16[4,8192]{1,0:T(4,128)(2,1)}, u32[]{:S(2)}) %copy-start.1) | copy-done | bytes 65560
  3.7 54.3 %shard_map.68 = (bf16[192,64,128]{2,1,0:T(8,128)(2,1)S(1)}, bf16[16,32,128]{2,1,0:T(8,128)(2,1)S(1)}, bf16[8,32,128]{2,1,0:T(8,128)(2,1)S(1)}) custom-call(s32[8,192]{1,0:T(8,128)S(1)} %select_reduce_fusion.inv_ref, bf16[8,24576]{1,0:T(8,128)(2,1)S(1)} %copy-done, bf16[8,32,128]{2,1,0:T(8,128)(2,1)S(1)} %bitcast.17, bf16[1024,128,128]{2,1,0:T(8,128)(2,1)} %bitcast.21), custom_call_target="tpu_custom_call" | custom-call | flops 3221225472 | bytes 39845888 | tf_op jit(solution)/shard_map/pallas_call | solution.py:383
  58.0 0.7 copy.16
  58.6 1.1 %copy.17.x_ref = bf16[8,128,64]{2,1,0:T(8,128)(2,1)S(1)} copy(bf16[8,128,64]{1,0,2:T(8,128)(2,1)} %bitcast.22) | data formatting | bytes 262144 | tf_op jit(solution)/shard_map/reshape | solution.py:429
  59.7 0.0 copy-done.2
  59.8 15.0 %shard_map.69 = bf16[8,128,128,128]{3,2,1,0:T(8,128)(2,1)} custom-call(s32[8,128]{1,0:T(8,128)S(1)} %get-tuple-element.9.idx_ref, s32[8]{0:T(128)S(1)} %bitcast.20, bf16[192,64,128]{2,1,0:T(8,128)(2,1)S(1)} %get-tuple-element.6.og_ref, bf16[8,128,64]{2,1,0:T(8,128)(2,1)S(1)} %copy.17.x_ref), custom_call_target="tpu_custom_call" | custom-call | tf_op jit(solution)/shard_map/pallas_call | solution.py:432
  74.8 0.6 copy.19
  (1 shorter events, 0.0 us)
Async XLA Ops:
  0.6 59.1 %copy-start.2 = (s32[8,1]{0,1:T(1,128)S(1)}, s32[8,1]{0,1:T(1,128)}, u32[]{:S(2)}) copy-start(s32[8,1]{0,1:T(1,128)} %param.8) | copy-start | bytes 100
  1.8 1.0 %copy-start = (bf16[8,24576]{1,0:T(8,128)(2,1)S(1)}, bf16[8,24576]{1,0:T(8,128)(2,1)}, u32[]{:S(2)}) copy-start(bf16[8,24576]{1,0:T(8,128)(2,1)} %og_ref.1) | copy-start | bytes 1179652
  2.8 0.8 %copy-start.1 = (bf16[4,8192]{1,0:T(4,128)(2,1)S(1)}, bf16[4,8192]{1,0:T(4,128)(2,1)}, u32[]{:S(2)}) copy-start(bf16[4,8192]{1,0:T(4,128)(2,1)} %param.5) | copy-start | bytes 196612
